TPU v7x, 512 devices: a whole 4x4x16 slice. The times are simulated.
512 devices in a mesh: span: 8 (over z_hi, y), stream: 64 (over x, z_lo, core).
Axes of the slice: x: 4, y: 4, z: 16 (z_hi: 2, z_lo: 8; z = z_hi * 8 + z_lo), core: 2. Of those that a mesh axis runs over, the one named last changes fastest.
Arguments:
- velocity: float32 [3, 32, 512, 256], P(None, 'span', 'stream'), may hold values from -32 to 32
- strain: float32 [6, 32, 512, 256], P(None, 'span', 'stream'), may hold values from -4 to 4
- row_bins: int32 [512], P('stream'), may hold values from 0 to 63, never falling along the last dimension, each value on 1 to 16 neighbouring positions
- cotangent: float32 [6, 32, 512, 256], P(None, 'span', 'stream'), may hold values from -6 to 6
Outputs:
- model_residual: float32 [6, 32, 512, 256], P(None, 'span', 'stream')
- velocity_grad: float32 [3, 32, 512, 256], P(None, 'span', 'stream')
Inputs may be any that keep to these rules, and one draw needn't show every extreme that they name: `row_bins`: bins never fall along the rows, and every bin holds 1 to 16 rows.
All inputs are finite; a program needn't handle non-finite values.
Results may differ from a plain program's by a relative error of at most 0.0003.
Values sent between devices are 32-bit elements; how exact they have to be, the bound alone decides.
A program may use at most 64 MiB of HBM per device.

v0:
```python
import jax
import jax.numpy as jnp
import numpy as np
from jax import lax
from jax.sharding import PartitionSpec as P

NBINS = 64
FILTER_ALPHA = 0.45
CENTER_WEIGHT = 0.95
SIDE_WEIGHT = 0.475
STRAIN_FLOOR = 0.25
EPSILON = 1e-06
INDEX_PAIRS = ((0, 0), (0, 1), (0, 2), (1, 1), (1, 2), (2, 2))
PAIR_WEIGHTS = (1.0, 2.0, 2.0, 1.0, 2.0, 1.0)
HIGHEST = lax.Precision.HIGHEST


def extended(array, sides, width):
    for axis, dim in sides:
        peers, length = (lax.axis_size(axis), array.shape[dim])
        up = [(i, (i + 1) % peers) for i in range(peers)]
        down = [(j, i) for i, j in up]
        last = lax.slice_in_dim(array, length - width, length, axis=dim)
        first = lax.slice_in_dim(array, 0, width, axis=dim)
        before = lax.ppermute(last, axis, up)
        after = lax.ppermute(first, axis, down)
        array = jnp.concatenate([before, array, after], axis=dim)
    return array


def invert_table(matrix):
    extent = matrix.shape[0]
    augmented = np.concatenate([np.array(matrix), np.eye(extent)], axis=1)
    for column in range(extent):
        pivot_row = column + int(np.argmax(np.abs(augmented[column:, column])))
        swapped = augmented[[pivot_row, column]]
        augmented[[column, pivot_row]] = swapped
        augmented[column] = augmented[column] / augmented[column, column]
        for row_index in range(extent):
            if row_index != column:
                augmented[row_index] = (
                    augmented[row_index] - augmented[row_index, column] * augmented[column]
                )
    return augmented[:, extent:]


def loop_tables(cell_count, devices):
    local_system = np.eye(cell_count) + FILTER_ALPHA * (
        np.eye(cell_count, k=1) + np.eye(cell_count, k=-1)
    )
    local_inverse = invert_table(local_system)
    first_column = local_inverse[:, 0]
    last_column = local_inverse[:, cell_count - 1]
    unknowns = 2 * devices
    coupling = np.eye(unknowns)
    for device in range(devices):
        previous = (device - 1) % devices
        following = (device + 1) % devices
        for which_end, cell_index in ((0, 0), (1, cell_count - 1)):
            target = 2 * device + which_end
            coupling[target, 2 * previous + 1] += FILTER_ALPHA * first_column[cell_index]
            coupling[target, 2 * following] += FILTER_ALPHA * last_column[cell_index]
    reduced = invert_table(coupling)
    selectors = np.stack(
        [
            reduced[[2 * ((device - 1) % devices) + 1, 2 * ((device + 1) % devices)], :]
            for device in range(devices)
        ]
    )
    return (
        jnp.asarray(local_inverse, jnp.float32),
        jnp.asarray(first_column, jnp.float32),
        jnp.asarray(last_column, jnp.float32),
        jnp.asarray(selectors, jnp.float32),
    )


def rim_side(values):
    padded = extended(values, (("span", 1),), 1)
    return CENTER_WEIGHT * values + SIDE_WEIGHT * (padded[:, 2:] + padded[:, :-2])


def solve_loop(values, tables, own_index):
    local_inverse, first_column, last_column, selectors = tables
    particular = jnp.einsum("ij,fjyx->fiyx", local_inverse, values, precision=HIGHEST)
    end_values = jnp.stack([particular[:, 0], particular[:, -1]], axis=0)
    selector = lax.dynamic_index_in_dim(selectors, own_index, 0, keepdims=False)
    gathered_piece = lax.all_gather(end_values, "span", axis=0, tiled=True)
    columns = lax.slice_in_dim(selector, 0, gathered_piece.shape[0], axis=1)
    neighbours = jnp.zeros_like(end_values) + jnp.einsum(
        "ae,efyx->afyx", columns, gathered_piece, precision=HIGHEST
    )
    previous = neighbours[0]
    following = neighbours[1]
    solved = particular - FILTER_ALPHA * (
        first_column[None, :, None, None] * previous[:, None]
        + last_column[None, :, None, None] * following[:, None]
    )
    return (solved, previous, following)


def solve_back(values, tables, own_index):
    local_inverse, first_column, last_column, selectors = tables
    selector = lax.dynamic_index_in_dim(selectors, own_index, 0, keepdims=False)
    near_bar = -FILTER_ALPHA * jnp.stack(
        [
            jnp.einsum("i,fiyx->fyx", first_column, values, precision=HIGHEST),
            jnp.einsum("i,fiyx->fyx", last_column, values, precision=HIGHEST),
        ],
        axis=0,
    )
    columns = lax.slice_in_dim(selector, 0, 2 * lax.axis_size("span"), axis=1)
    end_bar = lax.psum_scatter(
        jnp.einsum("ae,afyx->efyx", columns, near_bar, precision=HIGHEST),
        "span",
        scatter_dimension=0,
        tiled=True,
    )
    particular_bar = values.at[:, 0].add(end_bar[0]).at[:, -1].add(end_bar[1])
    return jnp.einsum("ji,fjyx->fiyx", local_inverse, particular_bar, precision=HIGHEST)


def smooth(values, tables, own_index):
    return solve_loop(rim_side(values), tables, own_index)[0]


def unsmooth(values, tables, own_index):
    return rim_side(solve_back(values, tables, own_index))


def on_device(velocity, strain, row_bins, cotangent):
    tables = loop_tables(velocity.shape[1], lax.axis_size("span"))
    own_index = lax.axis_index("span")
    weights = jnp.asarray(PAIR_WEIGHTS, jnp.float32)[:, None, None, None]
    products = jnp.stack([velocity[former] * velocity[latter] for former, latter in INDEX_PAIRS])
    size_field = jnp.sqrt(
        jnp.maximum(2.0 * jnp.sum(weights * strain * strain, axis=0), STRAIN_FLOOR)
    )
    fields = jnp.concatenate([velocity, products, size_field[None]], axis=0)
    filtered = smooth(fields, tables, own_index)
    coarse = jnp.stack([filtered[former] * filtered[latter] for former, latter in INDEX_PAIRS])
    leonard = filtered[3:9] - coarse
    model_term = products - coarse + 2.0 * (4.0 * filtered[9] - size_field)[None] * strain
    onehot = (row_bins[:, None] == jnp.arange(NBINS, dtype=jnp.int32)[None, :]).astype(jnp.float32)
    cross_local = jnp.dot(
        jnp.sum(weights * leonard * model_term, axis=(0, 1, 3)), onehot, precision=HIGHEST
    )
    square_local = jnp.dot(
        jnp.sum(weights * model_term * model_term, axis=(0, 1, 3)), onehot, precision=HIGHEST
    )
    blame_local = jnp.dot(
        jnp.sum(cotangent * model_term, axis=(0, 1, 3)), onehot, precision=HIGHEST
    )
    cross_bins, square_bins, blame_bins = lax.psum(
        (cross_local, square_local, blame_local), ("span", "stream")
    )
    denominator = square_bins + EPSILON
    coefficient = cross_bins / denominator
    row_coefficient = jnp.dot(onehot, coefficient, precision=HIGHEST)[None, None, :, None]
    residual = leonard - row_coefficient * model_term
    coefficient_bar = -blame_bins
    cross_bar = coefficient_bar / denominator
    square_bar = -coefficient_bar * coefficient / denominator
    row_cross = jnp.dot(onehot, cross_bar, precision=HIGHEST)[None, None, :, None]
    row_square = jnp.dot(onehot, square_bar, precision=HIGHEST)[None, None, :, None]
    leonard_bar = cotangent + row_cross * weights * model_term
    model_bar = (
        -row_coefficient * cotangent
        + row_cross * weights * leonard
        + 2.0 * row_square * weights * model_term
    )
    zero_field = jnp.zeros_like(velocity[0])
    coarse_bar = [zero_field, zero_field, zero_field]
    for position, (former, latter) in enumerate(INDEX_PAIRS):
        combined = leonard_bar[position] + model_bar[position]
        coarse_bar[former] = coarse_bar[former] - combined * filtered[latter]
        coarse_bar[latter] = coarse_bar[latter] - combined * filtered[former]
    pulled = unsmooth(
        jnp.concatenate([jnp.stack(coarse_bar), leonard_bar], axis=0), tables, own_index
    )
    gradient_parts = [pulled[0], pulled[1], pulled[2]]
    for position, (former, latter) in enumerate(INDEX_PAIRS):
        through = pulled[3 + position] + model_bar[position]
        gradient_parts[former] = gradient_parts[former] + through * velocity[latter]
        gradient_parts[latter] = gradient_parts[latter] + through * velocity[former]
    return (residual, jnp.stack(gradient_parts))


def solution(mesh):
    return jax.shard_map(
        on_device,
        mesh=mesh,
        in_specs=(
            P(None, "span", "stream", None),
            P(None, "span", "stream", None),
            P("stream"),
            P(None, "span", "stream", None),
        ),
        out_specs=(P(None, "span", "stream", None), P(None, "span", "stream", None)),
        check_vma=False,
    )
```

profile of v0, /device:TPU:130, one launch (start us, length us, event | category | flops | bytes accessed | tf_op | source)
XLA Modules:
  0.0 400.0 jit_solution(6443093883510731724)
XLA Ops:
  7.2 0.8 fusion.61
  8.0 0.9 constant_dynamic-update-slice_fusion.7
  8.9 1.1 fusion.10
  10.4 13.4 %collective-permute-start = (f32[10,1,8,256]{3,2,1,0:T(8,128)S(1)}, f32[10,1,8,256]{3,2,1,0:T(8,128)S(1)}, u32[]{:S(2)}, u32[]{:S(2)}) collective-permute-start(f32[10,1,8,256]{3,2,1,0:T(8,128)S(1)} %get-tuple-element.54), channel_id=1, source_target_pairs={{64,0},{128,64},{192,128},{256,192},{320,256},{384,320},{448,384},... | collective-permute-start | bytes 245768 | tf_op jit(solution)/shard_map/ppermute | solution.py:26
  23.7 1.9 collective-permute-start.1
  25.8 16.1 %collective-permute-done.1 = f32[10,1,8,256]{3,2,1,0:T(8,128)S(1)} collective-permute-done((f32[10,1,8,256]{3,2,1,0:T(8,128)S(1)}, f32[10,1,8,256]{3,2,1,0:T(8,128)S(1)}, u32[]{:S(2)}, u32[]{:S(2)}) %collective-permute-start.1) | collective-permute-done | bytes 81952 | tf_op jit(solution)/shard_map/ppermute | solution.py:25
  42.0 0.7 convolution_bitcast_fusion
  43.0 0.7 copy.44
  43.8 84.5 %all-gather.2.cloned.1.call-done = f32[16,10,8,256]{3,2,1,0:T(8,128)} async-done(((f32[2,10,8,256]{3,2,1,0:T(8,128)}), f32[16,10,8,256]{3,2,1,0:T(8,128)}) %all-gather.2.cloned.1.call-update) | async-done | bytes 1310736 | tf_op jit(solution)/shard_map/all_gather | solution.py:88
  128.3 2.7 fusion
  133.0 107.1 %all-reduce = (f32[64]{0:T(128)S(1)}, f32[64]{0:T(128)S(1)}, f32[64]{0:T(128)S(1)}) all-reduce(f32[64]{0:T(128)S(1)} %convolution_bitcast_fusion.7, f32[64]{0:T(128)S(1)} %convolution_bitcast_fusion.6, f32[64]{0:T(128)S(1)} %convolution_bitcast_fusion.4), channel_id=1, replica_groups=mesh['span'=8,'stream'=64] {'span','stream'}, use_global_device_ids=true, to_apply=%region_2.3 | all-reduce | flops 192 | bytes 1536 | tf_op jit(solution)/shard_map/psum | solution.py:154
  242.1 0.6 fusion.63
  242.8 1.9 fusion.12
  244.8 1.7 copy.50
  246.5 108.7 %reduce-scatter.2.cloned.1.call-done = f32[2,9,8,256]{3,2,1,0:T(8,128)} async-done(((f32[16,9,8,256]{3,2,1,0:T(8,128)}), f32[2,9,8,256]{3,2,1,0:T(8,128)}) %reduce-scatter.2.cloned.1.call-update) | async-done | bytes 147472 | tf_op jit(solution)/shard_map/reduce_scatter | solution.py:113
  355.2 0.9 fusion.60
  356.3 2.2 scatter-add.6
  358.6 2.2 scatter-add.9
  360.7 0.7 convolution_bitcast_fusion.1
  361.5 12.4 %collective-permute-start.2 = (f32[9,1,8,256]{3,1,2,0:T(1,128)S(1)}, f32[9,1,8,256]{3,1,2,0:T(1,128)S(1)}, u32[]{:S(2)}, u32[]{:S(2)}) collective-permute-start(f32[9,1,8,256]{3,1,2,0:T(1,128)S(1)} %get-tuple-element.56), channel_id=1, source_target_pairs={{64,0},{128,64},{192,128},{256,192},{320,256},{384,320},{448,384},... | collective-permute-start | bytes 221192 | tf_op jit(solution)/shard_map/ppermute | solution.py:26
  373.9 1.9 collective-permute-start.3
  375.9 0.7 copy.54
  376.6 15.4 %collective-permute-done.3 = f32[9,1,8,256]{3,1,2,0:T(1,128)S(1)} collective-permute-done((f32[9,1,8,256]{3,1,2,0:T(1,128)S(1)}, f32[9,1,8,256]{3,1,2,0:T(1,128)S(1)}, u32[]{:S(2)}, u32[]{:S(2)}) %collective-permute-start.3) | collective-permute-done | bytes 73760 | tf_op jit(solution)/shard_map/ppermute | solution.py:25
  392.5 0.7 copy.55
  (76 shorter events, 5.6 us)
Async XLA Ops:
  7.2 121.1 %all-gather.2.cloned.1.call-start = ((), (), s32[]{:S(2)}) async-start(), calls=%async_computation.1 | async-start | bytes 1474560 | tf_op jit(solution)/shard_map/all_gather | solution.py:88
  8.9 33.1 %copy-start.2 = (f32[4,4,1,1]{1,0,3,2:T(4,128)S(1)}, f32[4,4,1,1]{1,0,3,2:T(4,128)}, u32[]{:S(2)}) copy-start(f32[4,4,1,1]{1,0,3,2:T(4,128)} %constant.110) | copy-start | bytes 196
  10.4 15.4 %collective-permute-start = (f32[10,1,8,256]{3,2,1,0:T(8,128)S(1)}, f32[10,1,8,256]{3,2,1,0:T(8,128)S(1)}, u32[]{:S(2)}, u32[]{:S(2)}) collective-permute-start(f32[10,1,8,256]{3,2,1,0:T(8,128)S(1)} %get-tuple-element.54), channel_id=1, source_target_pairs={{64,0},{128,64},{192,128},{256,192},{320,256},{384,320},{448,384},... | collective-permute-start | bytes 245768 | tf_op jit(solution)/shard_map/ppermute | solution.py:26
  23.7 18.2 %collective-permute-start.1 = (f32[10,1,8,256]{3,2,1,0:T(8,128)S(1)}, f32[10,1,8,256]{3,2,1,0:T(8,128)S(1)}, u32[]{:S(2)}, u32[]{:S(2)}) collective-permute-start(f32[10,1,8,256]{3,2,1,0:T(8,128)S(1)} %get-tuple-element.55), channel_id=1, source_target_pairs={{0,64},{64,128},{128,192},{192,256},{256,320},{320,384},{384,448},... | collective-permute-start | bytes 245768 | tf_op jit(solution)/shard_map/ppermute | solution.py:25
  43.0 88.2 %copy-start.6 = (f32[4]{0:T(128)S(1)}, f32[4]{0:T(128)}, u32[]{:S(2)}) copy-start(f32[4]{0:T(128)} %constant.103.clone) | copy-start | bytes 52
  43.0 88.2 %copy-start.7 = (f32[4]{0:T(128)S(1)}, f32[4]{0:T(128)}, u32[]{:S(2)}) copy-start(f32[4]{0:T(128)} %constant.102.clone) | copy-start | bytes 52
  43.7 311.5 %reduce-scatter.2.cloned.1.call-start = ((), (), s32[]{:S(2)}) async-start(), calls=%async_computation.2 | async-start | bytes 1327104 | tf_op jit(solution)/shard_map/reduce_scatter | solution.py:113
  131.0 0.9 copy-start
  131.0 1.0 copy-start.1
  131.0 1.0 copy-start.3
  131.2 1.2 copy-start.8
  240.7 0.7 copy-start.5
  241.0 1.1 copy-start.4
  361.5 15.1 %collective-permute-start.2 = (f32[9,1,8,256]{3,1,2,0:T(1,128)S(1)}, f32[9,1,8,256]{3,1,2,0:T(1,128)S(1)}, u32[]{:S(2)}, u32[]{:S(2)}) collective-permute-start(f32[9,1,8,256]{3,1,2,0:T(1,128)S(1)} %get-tuple-element.56), channel_id=1, source_target_pairs={{64,0},{128,64},{192,128},{256,192},{320,256},{384,320},{448,384},... | collective-permute-start | bytes 221192 | tf_op jit(solution)/shard_map/ppermute | solution.py:26
  373.9 18.0 %collective-permute-start.3 = (f32[9,1,8,256]{3,1,2,0:T(1,128)S(1)}, f32[9,1,8,256]{3,1,2,0:T(1,128)S(1)}, u32[]{:S(2)}, u32[]{:S(2)}) collective-permute-start(f32[9,1,8,256]{3,1,2,0:T(1,128)S(1)} %get-tuple-element.57), channel_id=1, source_target_pairs={{0,64},{64,128},{128,192},{192,256},{256,320},{320,384},{384,448},... | collective-permute-start | bytes 221192 | tf_op jit(solution)/shard_map/ppermute | solution.py:25
Sparse Core Ops, SparseCore 0:
  43.9 84.3 all-gather.1
  246.6 108.5 reduce-scatter.1
where the time goes:
time: 400 us
  waiting for transfers between devices  225 us (56%)
  blocking collectives  107 us (27%)
  starting transfers between devices  29.7 us (7%)
  between operations  14.5 us (4%)
  local copies, waits for them, and re-layouts  12 us (3%)
  matrix products  8.42 us (2%)
    reduce_scatter x1, waiting for transfers between devices, solve_back(): lax.psum_scatter(jnp.einsum('ae,afyx->efyx', columns, near_bar, precision...  109 us
    psum x1, blocking collectives, on_device(): lax.psum((cross_local, square_local, blame_local), ('span', 'stream'))  107 us
    all_gather x1, waiting for transfers between devices, solve_loop(): gathered_piece = lax.all_gather(end_values, 'span', axis=0, tiled=True)  84.5 us
    ppermute x2, waiting for transfers between devices, extended(): before = lax.ppermute(last, axis, up)  31.5 us
    ppermute x2, starting transfers between devices, extended(): after = lax.ppermute(first, axis, down)  25.8 us
  transfers between devices with their start and end apart: 6, of which 6 were waited for; matrix products, arithmetic and copies ran while one was open for 0% of the time, Pallas kernels for 0%

commit v1 on v0

--- a/solution.py
+++ b/solution.py
@@ -13,6 +13,11 @@
 INDEX_PAIRS = ((0, 0), (0, 1), (0, 2), (1, 1), (1, 2), (2, 2))
 PAIR_WEIGHTS = (1.0, 2.0, 2.0, 1.0, 2.0, 1.0)
 HIGHEST = lax.Precision.HIGHEST
+
+
+def gather_over(x, axis, d):
+    repeated = jnp.stack([x] * lax.axis_size(axis))
+    return jnp.concatenate(lax.all_to_all(repeated, axis, 0, 0), axis=d)
 
 
 def extended(array, sides, width):
@@ -85,7 +90,7 @@
     particular = jnp.einsum("ij,fjyx->fiyx", local_inverse, values, precision=HIGHEST)
     end_values = jnp.stack([particular[:, 0], particular[:, -1]], axis=0)
     selector = lax.dynamic_index_in_dim(selectors, own_index, 0, keepdims=False)
-    gathered_piece = lax.all_gather(end_values, "span", axis=0, tiled=True)
+    gathered_piece = gather_over(end_values, "span", 0)
     columns = lax.slice_in_dim(selector, 0, gathered_piece.shape[0], axis=1)
     neighbours = jnp.zeros_like(end_values) + jnp.einsum(
         "ae,efyx->afyx", columns, gathered_piece, precision=HIGHEST

time: 400 us -> 386 us (0.965)
  the two profiles are of different devices: /device:TPU:130 before, /device:TPU:128 now
where the time goes in v1:
time: 386 us; the launch traced here: 385 us
  waiting for transfers between devices  195 us (51%)
  blocking collectives  117 us (30%)
  starting transfers between devices  34 us (9%)
  local copies, waits for them, and re-layouts  14.7 us (4%)
  between operations  14.5 us (4%)
  matrix products  7.11 us (2%)
    psum x1, blocking collectives, on_device(): lax.psum((cross_local, square_local, blame_local), ('span', 'stream'))  117 us
    reduce_scatter x1, waiting for transfers between devices, solve_back(): lax.psum_scatter(jnp.einsum('ae,afyx->efyx', columns, near_bar, precision...  110 us
    all_to_all x1, waiting for transfers between devices, gather_over(): return jnp.concatenate(lax.all_to_all(repeated, axis, 0, 0), axis=d)  53 us
    ppermute x2, waiting for transfers between devices, extended(): before = lax.ppermute(last, axis, up)  31.3 us
    ppermute x2, starting transfers between devices, extended(): after = lax.ppermute(first, axis, down)  25.7 us
  transfers between devices with their start and end apart: 6, of which 6 were waited for; matrix products, arithmetic and copies ran while one was open for 0% of the time, Pallas kernels for 0%

profile of v1, /device:TPU:128, one launch (start us, length us, event | category | flops | bytes accessed | tf_op | source)
XLA Modules:
  0.0 385.4 jit_solution(17453425284992110512)
XLA Ops:
  7.2 0.8 fusion.60
  8.0 0.9 constant_dynamic-update-slice_fusion.7
  9.1 1.1 fusion.8
  10.3 13.4 %collective-permute-start = (f32[10,1,8,256]{3,2,1,0:T(8,128)S(1)}, f32[10,1,8,256]{3,2,1,0:T(8,128)S(1)}, u32[]{:S(2)}, u32[]{:S(2)}) collective-permute-start(f32[10,1,8,256]{3,2,1,0:T(8,128)S(1)} %get-tuple-element.54), channel_id=1, source_target_pairs={{64,0},{128,64},{192,128},{256,192},{320,256},{384,320},{448,384},... | collective-permute-start | bytes 245768 | tf_op jit(solution)/shard_map/ppermute | solution.py:31
  23.7 1.9 collective-permute-start.1
  25.7 16.1 %collective-permute-done.1 = f32[10,1,8,256]{3,2,1,0:T(8,128)S(1)} collective-permute-done((f32[10,1,8,256]{3,2,1,0:T(8,128)S(1)}, f32[10,1,8,256]{3,2,1,0:T(8,128)S(1)}, u32[]{:S(2)}, u32[]{:S(2)}) %collective-permute-start.1) | collective-permute-done | bytes 81952 | tf_op jit(solution)/shard_map/ppermute | solution.py:30
  41.9 0.7 convolution_bitcast_fusion
  43.0 1.7 stack.17
  44.7 4.3 %all-to-all-start = ((f32[8,2,10,8,256]{4,1,3,2,0:T(2,128)}), f32[8,2,10,8,256]{4,1,3,2,0:T(2,128)S(1)}, u32[]{:S(2)}, u32[]{:S(2)}) async-start(f32[8,2,10,8,256]{4,1,3,2,0:T(2,128)} %stack.17), calls=%async_computation | async-start | bytes 2621440 | tf_op jit(solution)/shard_map/all_to_all | solution.py:20
  49.1 53.0 %all-to-all-done = f32[8,2,10,8,256]{4,1,3,2,0:T(2,128)S(1)} async-done(((f32[8,2,10,8,256]{4,1,3,2,0:T(2,128)}), f32[8,2,10,8,256]{4,1,3,2,0:T(2,128)S(1)}, u32[]{:S(2)}, u32[]{:S(2)}) %all-to-all-start) | async-done | bytes 1310752 | tf_op jit(solution)/shard_map/all_to_all | solution.py:20
  102.1 0.7 copy.44
  102.8 0.9 reshape.166
  103.7 1.4 fusion.37
  107.2 116.7 %all-reduce = (f32[64]{0:T(128)S(1)}, f32[64]{0:T(128)S(1)}, f32[64]{0:T(128)S(1)}) all-reduce(f32[64]{0:T(128)S(1)} %convolution_bitcast_fusion.7, f32[64]{0:T(128)S(1)} %convolution_bitcast_fusion.6, f32[64]{0:T(128)S(1)} %convolution_bitcast_fusion.4), channel_id=1, replica_groups=mesh['span'=8,'stream'=64] {'span','stream'}, use_global_device_ids=true, to_apply=%region_2.3 | all-reduce | flops 192 | bytes 1536 | tf_op jit(solution)/shard_map/psum | solution.py:159
  226.5 1.9 fusion.10
  228.5 1.7 copy.49
  230.3 110.2 %reduce-scatter.2.cloned.1.call-done = f32[2,9,8,256]{3,2,1,0:T(8,128)} async-done(((f32[16,9,8,256]{3,2,1,0:T(8,128)}), f32[2,9,8,256]{3,2,1,0:T(8,128)}) %reduce-scatter.2.cloned.1.call-update) | async-done | bytes 147472 | tf_op jit(solution)/shard_map/reduce_scatter | solution.py:118
  340.5 0.9 fusion.59
  341.5 2.2 scatter-add.6
  343.8 2.2 scatter-add.9
  346.8 12.4 %collective-permute-start.2 = (f32[9,1,8,256]{3,1,2,0:T(1,128)S(1)}, f32[9,1,8,256]{3,1,2,0:T(1,128)S(1)}, u32[]{:S(2)}, u32[]{:S(2)}) collective-permute-start(f32[9,1,8,256]{3,1,2,0:T(1,128)S(1)} %get-tuple-element.56), channel_id=1, source_target_pairs={{64,0},{128,64},{192,128},{256,192},{320,256},{384,320},{448,384},... | collective-permute-start | bytes 221192 | tf_op jit(solution)/shard_map/ppermute | solution.py:31
  359.2 1.9 collective-permute-start.3
  361.1 0.7 copy.53
  362.2 15.2 %collective-permute-done.3 = f32[9,1,8,256]{3,1,2,0:T(1,128)S(1)} collective-permute-done((f32[9,1,8,256]{3,1,2,0:T(1,128)S(1)}, f32[9,1,8,256]{3,1,2,0:T(1,128)S(1)}, u32[]{:S(2)}, u32[]{:S(2)}) %collective-permute-start.3) | collective-permute-done | bytes 73760 | tf_op jit(solution)/shard_map/ppermute | solution.py:30
  (77 shorter events, 7.9 us)
Async XLA Ops:
  8.9 33.1 %copy-start.2 = (f32[4,4,1,1]{1,0,3,2:T(4,128)S(1)}, f32[4,4,1,1]{1,0,3,2:T(4,128)}, u32[]{:S(2)}) copy-start(f32[4,4,1,1]{1,0,3,2:T(4,128)} %constant.110) | copy-start | bytes 196
  10.3 15.4 %collective-permute-start = (f32[10,1,8,256]{3,2,1,0:T(8,128)S(1)}, f32[10,1,8,256]{3,2,1,0:T(8,128)S(1)}, u32[]{:S(2)}, u32[]{:S(2)}) collective-permute-start(f32[10,1,8,256]{3,2,1,0:T(8,128)S(1)} %get-tuple-element.54), channel_id=1, source_target_pairs={{64,0},{128,64},{192,128},{256,192},{320,256},{384,320},{448,384},... | collective-permute-start | bytes 245768 | tf_op jit(solution)/shard_map/ppermute | solution.py:31
  23.7 18.2 %collective-permute-start.1 = (f32[10,1,8,256]{3,2,1,0:T(8,128)S(1)}, f32[10,1,8,256]{3,2,1,0:T(8,128)S(1)}, u32[]{:S(2)}, u32[]{:S(2)}) collective-permute-start(f32[10,1,8,256]{3,2,1,0:T(8,128)S(1)} %get-tuple-element.55), channel_id=1, source_target_pairs={{0,64},{64,128},{128,192},{192,256},{256,320},{320,384},{384,448},... | collective-permute-start | bytes 245768 | tf_op jit(solution)/shard_map/ppermute | solution.py:30
  44.7 57.4 %all-to-all-start = ((f32[8,2,10,8,256]{4,1,3,2,0:T(2,128)}), f32[8,2,10,8,256]{4,1,3,2,0:T(2,128)S(1)}, u32[]{:S(2)}, u32[]{:S(2)}) async-start(f32[8,2,10,8,256]{4,1,3,2,0:T(2,128)} %stack.17), calls=%async_computation | async-start | bytes 2621440 | tf_op jit(solution)/shard_map/all_to_all | solution.py:20
  49.0 291.4 %reduce-scatter.2.cloned.1.call-start = ((), (), s32[]{:S(2)}) async-start(), calls=%async_computation.2 | async-start | bytes 1327104 | tf_op jit(solution)/shard_map/reduce_scatter | solution.py:118
  103.7 1.7 copy-start.6
  103.7 1.7 copy-start.7
  105.2 0.9 copy-start
  105.2 1.0 copy-start.1
  105.2 1.0 copy-start.3
  105.4 1.2 copy-start.8
  224.5 0.7 copy-start.5
  224.7 1.1 copy-start.4
  346.8 15.4 %collective-permute-start.2 = (f32[9,1,8,256]{3,1,2,0:T(1,128)S(1)}, f32[9,1,8,256]{3,1,2,0:T(1,128)S(1)}, u32[]{:S(2)}, u32[]{:S(2)}) collective-permute-start(f32[9,1,8,256]{3,1,2,0:T(1,128)S(1)} %get-tuple-element.56), channel_id=1, source_target_pairs={{64,0},{128,64},{192,128},{256,192},{320,256},{384,320},{448,384},... | collective-permute-start | bytes 221192 | tf_op jit(solution)/shard_map/ppermute | solution.py:31
  359.2 18.2 %collective-permute-start.3 = (f32[9,1,8,256]{3,1,2,0:T(1,128)S(1)}, f32[9,1,8,256]{3,1,2,0:T(1,128)S(1)}, u32[]{:S(2)}, u32[]{:S(2)}) collective-permute-start(f32[9,1,8,256]{3,1,2,0:T(1,128)S(1)} %get-tuple-element.57), channel_id=1, source_target_pairs={{0,64},{64,128},{128,192},{192,256},{256,320},{320,384},{384,448},... | collective-permute-start | bytes 221192 | tf_op jit(solution)/shard_map/ppermute | solution.py:30
Sparse Core Ops, SparseCore 0:
  230.4 110.0 reduce-scatter.1
